TPU v7x, 32 devices: a whole 2x2x4 slice. The times are simulated.
32 devices in a mesh: rows: 8 (over y, x, core), feat: 4 (over z).
Axes of the slice: x: 2, y: 2, z: 4, core: 2. Of those that a mesh axis runs over, the one named last changes fastest.
Arguments:
- node_feats: bfloat16 [256, 32768], P('feat', 'rows'), may hold values from -6 to 6
- tile_vals: bfloat16 [256, 16, 128, 128], P('rows'), may hold values from -0.125 to 0.125
- tile_cols: int32 [256, 16], P('rows'), may hold values from 0 to 255, as said below
- weight: bfloat16 [256, 256], P(None, 'feat'), may hold values from -0.375 to 0.375
- bias_vec: float32 [256], P('feat'), may hold values from -3 to 3
- grad_out: bfloat16 [256, 32768], P('feat', 'rows'), may hold values from -6 to 6
Outputs:
- activated: bfloat16 [256, 32768], P('feat', 'rows')
- grad_feats: float32 [256, 32768], P('feat', 'rows')
- grad_weight: float32 [256, 256], P(None, 'feat')
- grad_bias: float32 [256], P('feat')
Inputs may be any that keep to these rules, and one draw needn't show every extreme that they name: `tile_cols`: among the tiles of one device's 32 blocks of rows, the column blocks held by any one owner (blocks o * 32 to o * 32 + 31) are at most 16 distinct ones and at least one; on every device some owner reaches 16.
All inputs are finite; a program needn't handle non-finite values.
Results may differ from a plain program's by a relative error of at most 0.007.
Values may be sent and summed in bfloat16 or wider, within the bound.
A program may use at most 256 MiB of HBM per device.

v0:
```python
import jax
import jax.numpy as jnp
from jax import lax
from jax.sharding import PartitionSpec as P


def on_device(node_feats, tile_vals, tile_cols, weight, bias_vec, grad_out):
    feat_loc = node_feats.shape[0]
    own_blocks = tile_cols.shape[0]
    slots_per = tile_cols.shape[1]
    tile_edge = tile_vals.shape[2]
    row_devs = lax.axis_size("rows")
    flat_cols = tile_cols.reshape(-1)
    whole = lax.all_gather(node_feats, "rows", axis=1, tiled=True)
    picked = jnp.take(whole.reshape(feat_loc, -1, tile_edge), flat_cols, axis=1)
    picked = picked.reshape(feat_loc, own_blocks, slots_per, tile_edge)
    aggregated = jnp.einsum("fisb,isab->fia", picked, tile_vals, preferred_element_type=jnp.float32)
    aggregated = aggregated.reshape(feat_loc, own_blocks * tile_edge).astype(jnp.bfloat16)
    agg_all = lax.all_gather(aggregated, "feat", axis=0, tiled=True)
    preact = (
        lax.dot_general(
            weight, agg_all, (((0,), (0,)), ((), ())), preferred_element_type=jnp.float32
        )
        + bias_vec[:, None]
    )
    sigma = jax.nn.sigmoid(preact)
    activated = (preact * sigma).astype(jnp.bfloat16)
    grad_pre = (grad_out.astype(jnp.float32) * sigma * (1.0 + preact * (1.0 - sigma))).astype(
        jnp.bfloat16
    )
    weight_part = lax.dot_general(
        agg_all, grad_pre, (((1,), (1,)), ((), ())), preferred_element_type=jnp.float32
    )
    bias_part = jnp.sum(grad_pre.astype(jnp.float32), axis=1)
    grad_weight, grad_bias = lax.psum((weight_part, bias_part), "rows")
    back_mix = lax.psum_scatter(
        jnp.dot(weight, grad_pre, preferred_element_type=jnp.float32),
        "feat",
        scatter_dimension=0,
        tiled=True,
    )
    back_mix = back_mix.astype(jnp.bfloat16)
    contrib = jnp.einsum(
        "fia,isab->fisb",
        back_mix.reshape(feat_loc, own_blocks, tile_edge),
        tile_vals,
        preferred_element_type=jnp.float32,
    )
    contrib = contrib.reshape(feat_loc, own_blocks * slots_per, tile_edge)
    terms = (
        jnp.zeros((feat_loc, row_devs * own_blocks, tile_edge), jnp.float32)
        .at[:, flat_cols]
        .add(contrib)
    )
    grad_feats = lax.psum_scatter(
        terms.reshape(feat_loc, -1), "rows", scatter_dimension=1, tiled=True
    )
    return (activated, grad_feats, grad_weight, grad_bias)


def solution(mesh):
    placed = (
        P("feat", "rows"),
        P("rows", None, None, None),
        P("rows", None),
        P(None, "feat"),
        P("feat"),
        P("feat", "rows"),
    )
    return jax.shard_map(
        on_device,
        mesh=mesh,
        in_specs=placed,
        out_specs=(P("feat", "rows"), P("feat", "rows"), P(None, "feat"), P("feat")),
        check_vma=False,
    )
```

profile of v0, /device:TPU:0, one launch (start us, length us, event | category | flops | bytes accessed | tf_op | source)
XLA Modules:
  0.0 407.5 jit_solution(2895431912800540972)
XLA Ops:
  7.2 0.0 copy-start
  7.2 0.0 all-gather.3.cloned.1.call-start
  7.2 0.7 all-gather.3.cloned.1.call-update
  7.9 0.0 all-gather.5.cloned.1.call-start
  8.0 0.8 copy.25
  8.7 0.7 compare_and_fusion
  9.4 0.1 copy.24
  9.5 0.1 reshape.64
  9.6 39.7 %all-gather.3.cloned.1.call-done = bf16[64,32768]{1,0:T(8,128)(2,1)} async-done(((bf16[64,4096]{1,0:T(8,128)(2,1)}), bf16[64,32768]{1,0:T(8,128)(2,1)}) %all-gather.3.cloned.1.call-update) | async-done | bytes 4194320 | tf_op jit(solution)/shard_map/all_gather | solution.py:14
  49.4 5.3 %copy_bitcast_fusion.1 = bf16[64,256,128]{2,0,1:T(8,128)(2,1)} fusion(bf16[64,32768]{1,0:T(8,128)(2,1)} %all-gather.3.cloned.1.call-done), kind=kLoop, calls=%fused_computation.9 | loop fusion | bytes 8388608 | tf_op jit(solution)/shard_map/reshape | solution.py:15
  54.7 21.8 %gather_fusion = bf16[512,64,128]{2,1,0:T(8,128)(2,1)} fusion(bf16[64,256,128]{2,0,1:T(8,128)(2,1)} %copy_bitcast_fusion.1, s32[1024]{0:T(1024)S(1)} %pad_clamp_fusion), kind=kCustom, calls=%fused_computation | custom fusion | bytes 16779264 | tf_op jit(solution)/shard_map/jit(_take)/gather | solution.py:15
  76.5 0.0 copy-start.3
  76.6 0.0 copy-start.4
  76.6 11.4 %fusion.11 = bf16[32,8,8,128]{3,2,1,0:T(8,128)(2,1)S(1)} fusion(bf16[32,16,128,128]{3,2,1,0:T(8,128)(2,1)} %param.7, bf16[64,32,16,128]{3,0,2,1:T(8,128)(2,1)} %bitcast.52, pred[32,16]{1,0:T(8,128)(4,1)S(1)} %copy.24), kind=kOutput, calls=%fused_computation.13 | convolution fusion | flops 1078198272 | bytes 25690624 | tf_op jit(solution)/shard_map/fisb,isab->fia/dot_general | solution.py:17
  88.0 0.9 copy.42
  88.9 0.0 all-gather.5.cloned.1.call-update
  88.9 0.0 reduce-scatter.7.cloned.1.call-start
  89.0 46.0 %all-gather.5.cloned.1.call-done = bf16[256,4096]{1,0:T(8,128)(2,1)} async-done(((bf16[64,4096]{1,0:T(8,128)(2,1)}), bf16[256,4096]{1,0:T(8,128)(2,1)}) %all-gather.5.cloned.1.call-update) | async-done | bytes 2097168 | tf_op jit(solution)/shard_map/all_gather | solution.py:19
  135.0 0.0 copy-done
  135.0 0.0 copy-done.3
  135.0 0.0 copy-done.4
  135.0 3.3 convert_reduce_fusion
  138.3 0.0 copy-start.2
  138.3 2.7 convolution_bitcast_fusion
  141.0 5.6 %copy.34 = f32[256,4096]{1,0:T(8,128)} copy(f32[256,4096]{0,1:T(8,128)} %convolution_bitcast_fusion) | data formatting | bytes 8388608
  146.7 0.0 reduce-scatter.7.cloned.1.call-update
  146.7 0.2 all-reduce.2.cloned.1.call-start
  146.9 0.0 copy-done.2
  146.9 1.4 fusion.16
  148.3 0.0 all-reduce.2.cloned.1.call-update
  148.4 0.0 reduce-scatter.5.cloned.1.call-start
  148.4 74.0 %reduce-scatter.7.cloned.1.call-done = f32[64,4096]{1,0:T(8,128)} async-done(((f32[256,4096]{1,0:T(8,128)}), f32[64,4096]{1,0:T(8,128)}) %reduce-scatter.7.cloned.1.call-update) | async-done | bytes 1048592
  222.4 1.7 copy.35
  224.1 14.0 %fusion.15 = f32[32,64,16,128]{3,1,2,0:T(8,128)} fusion(bf16[64,32,128,1]{0,2,3,1:T(8,128)(2,1)S(1)} %bitcast.53, bf16[32,16,128,128]{3,2,1,0:T(8,128)(2,1)} %param.7), kind=kOutput, calls=%fused_computation.24 | convolution fusion | flops 1073741824 | bytes 34078720 | tf_op jit(solution)/shard_map/fia,isab->fisb/dot_general | solution.py:43
  238.1 4.3 %broadcast_in_dim.17 = f32[64,256,128]{2,0,1:T(8,128)} broadcast(f32[]{:T(128)} %constant.22.clone.1), dimensions={} | broadcast | bytes 8388612 | tf_op jit(solution)/shard_map/broadcast_in_dim | solution.py:51
  242.4 78.1 %scatter_fusion = f32[64,256,128]{2,0,1:T(8,128)} fusion(f32[64,256,128]{2,0,1:T(8,128)} %broadcast_in_dim.17, s32[512]{0:T(512)S(1)} %bitcast.56, f32[512,64,128]{2,1,0:T(8,128)} %bitcast.51), kind=kCustom, calls=%fused_computation.1 | custom fusion | flops 4194304 | bytes 50333696 | tf_op jit(solution)/shard_map/scatter-add | solution.py:53
  320.5 0.0 copy-start.1
  320.5 7.1 %copy_bitcast_fusion = f32[64,32768]{1,0:T(8,128)} fusion(f32[64,256,128]{2,0,1:T(8,128)} %scatter_fusion), kind=kLoop, calls=%fused_computation.2 | loop fusion | bytes 16777216 | tf_op jit(solution)/shard_map/reshape | solution.py:56
  327.6 0.0 reduce-scatter.5.cloned.1.call-update
  327.7 14.1 %psum.15 = f32[64]{0:T(128)} all-reduce(f32[64]{0:T(128)S(1)} %get-tuple-element.4), channel_id=1, replica_groups=mesh['rows'=8,'feat'=4] {'rows'}, use_global_device_ids=true, to_apply=%region_5.6 | all-reduce | flops 64 | bytes 512 | tf_op jit(solution)/shard_map/psum | solution.py:35
  341.8 0.0 all-reduce.2.cloned.1.call-done
  341.8 57.7 %reduce-scatter.5.cloned.1.call-done = f32[64,4096]{1,0:T(8,128)} async-done(((f32[64,32768]{1,0:T(8,128)}), f32[64,4096]{1,0:T(8,128)}) %reduce-scatter.5.cloned.1.call-update) | async-done | bytes 1048592 | tf_op jit(solution)/shard_map/reduce_scatter | solution.py:55
  399.5 1.5 copy.45
  401.0 0.0 copy-done.1
  (2 shorter events, 0.0 us)
Async XLA Ops:
  7.2 127.8 %copy-start = (bf16[256,64]{0,1:T(8,128)(2,1)S(1)}, bf16[256,64]{0,1:T(8,128)(2,1)}, u32[]{:S(2)}) copy-start(bf16[256,64]{0,1:T(8,128)(2,1)} %param.9) | copy-start | bytes 98308
  7.2 42.2 %all-gather.3.cloned.1.call-start = ((), (), s32[]{:S(2)}) async-start(), calls=%async_computation.2 | async-start | bytes 4718592 | tf_op jit(solution)/shard_map/all_gather | solution.py:14
  7.9 127.1 %all-gather.5.cloned.1.call-start = ((), (), s32[]{:S(2)}) async-start(), calls=%async_computation.3 | async-start | bytes 2621440 | tf_op jit(solution)/shard_map/all_gather | solution.py:19
  76.5 58.5 %copy-start.3 = (bf16[64,4096]{1,0:T(8,128)(2,1)S(1)}, bf16[64,4096]{1,0:T(8,128)(2,1)}, u32[]{:S(2)}) copy-start(bf16[64,4096]{1,0:T(8,128)(2,1)} %param.11) | copy-start | bytes 1572868
  76.6 58.4 %copy-start.4 = (f32[64]{0:T(128)S(1)}, f32[64]{0:T(128)}, u32[]{:S(2)}) copy-start(f32[64]{0:T(128)} %param.10) | copy-start | bytes 772
  88.9 133.4 %reduce-scatter.7.cloned.1.call-start = ((), (), s32[]{:S(2)}) async-start(), calls=%async_computation.6 | async-start | bytes 5242880
  138.3 8.6 %copy-start.2 = (bf16[256,4096]{1,0:T(8,128)(2,1)S(1)}, bf16[256,4096]{1,0:T(8,128)(2,1)}, u32[]{:S(2)}) copy-start(bf16[256,4096]{1,0:T(8,128)(2,1)} %all-gather.5.cloned.1.call-done) | copy-start | bytes 6291460
  146.7 195.1 %all-reduce.2.cloned.1.call-start = ((), (), s32[]{:S(2)}) async-start(), calls=%async_computation.5 | async-start | bytes 131072 | tf_op jit(solution)/shard_map/psum | solution.py:35
  148.4 251.1 %reduce-scatter.5.cloned.1.call-start = ((), (), s32[]{:S(2)}) async-start(), calls=%async_computation.4 | async-start | bytes 9437184 | tf_op jit(solution)/shard_map/reduce_scatter | solution.py:55
  320.5 80.5 %copy-start.1 = (bf16[256,64]{0,1:T(8,128)(2,1)S(1)}, bf16[256,64]{0,1:T(8,128)(2,1)}, u32[]{:S(2)}) copy-start(bf16[256,64]{0,1:T(8,128)(2,1)} %param.9) | copy-start | bytes 98308
Sparse Core Ops, SparseCore 0:
  9.9 39.4 all-gather.2
  89.0 45.9 all-gather.4
  146.8 75.4 reduce-scatter.6
  226.1 52.9 all-reduce.1
  327.8 71.6 reduce-scatter.4
where the time goes:
time: 409 us; the launch traced here: 407 us
  waiting for transfers between devices  218 us (53%)
  other arithmetic  78.8 us (19%)
  local copies, waits for them, and re-layouts  49.3 us (12%)
  matrix products  32.8 us (8%)
  blocking collectives  14.1 us (3%)
  between operations  13.9 us (3%)
    scatter-add x1, other arithmetic, on_device(): terms = jnp.zeros((feat_loc, row_devs * own_blocks, tile_edge), jnp.float...  78.1 us
    unnamed x6, waiting for transfers between devices  74.7 us
    reduce_scatter x1, waiting for transfers between devices, on_device(): lax.psum_scatter(terms.reshape(feat_loc, -1), 'rows', scatter_dimension=1...  57.7 us
    all_gather x1, waiting for transfers between devices, on_device(): agg_all = lax.all_gather(aggregated, 'feat', axis=0, tiled=True)  46 us
    all_gather x1, waiting for transfers between devices, on_device(): whole = lax.all_gather(node_feats, 'rows', axis=1, tiled=True)  39.7 us
    gather x1, local copies, waits for them, and re-layouts, on_device(): picked = jnp.take(whole.reshape(feat_loc, -1, tile_edge), flat_cols, axis=1)  21.8 us
    psum x1, blocking collectives, on_device(): grad_weight, grad_bias = lax.psum((weight_part, bias_part), 'rows')  14.1 us
    dot_general x1, matrix products, on_device(): jnp.einsum('fia,isab->fisb', back_mix.reshape(feat_loc, own_blocks, tile_...  14 us
  transfers between devices with their start and end apart: 5, of which 4 were waited for; matrix products, arithmetic and copies ran while one was open for 27% of the time, Pallas kernels for 0%

commit v1 on v0

v1 whole, which is shorter than its diff:
```python
import functools

import jax
import jax.numpy as jnp
from jax import lax
from jax.experimental import pallas as pl
from jax.experimental.pallas import tpu as pltpu
from jax.sharding import PartitionSpec as P

MESH = pl.DeviceIdType.MESH
BF16 = jnp.bfloat16
F32 = jnp.float32
VMEM_BYTES = 60 * 1024 * 1024


def flip(index, mask, count):
    out, place = 0, 1
    while place < count:
        bit = (index // place) % 2
        out = out + ((1 - bit) if mask & place else bit) * place
        place *= 2
    return out


def greet(rows_peers, feat_peers):
    barrier = pltpu.get_barrier_semaphore()
    for peer in rows_peers:
        pl.semaphore_signal(barrier, inc=1, device_id={"rows": peer}, device_id_type=MESH)
    for peer in feat_peers:
        pl.semaphore_signal(barrier, inc=1, device_id={"feat": peer}, device_id_type=MESH)
    pl.semaphore_wait(barrier, len(rows_peers) + len(feat_peers))


def remote(src, dst, send_sem, recv_sem, **where):
    return pltpu.make_async_remote_copy(
        src_ref=src, dst_ref=dst, send_sem=send_sem, recv_sem=recv_sem,
        device_id=where, device_id_type=MESH,
    )


def forward_kernel(
    n_rows, n_feat,
    cols_ref, x_ref, gout_ref, wt_ref, bias_ref, tiles_hbm,
    bm_in, act_out, gw_ref, gb_ref,
    xall, gsend, gall, wall, ball, tiles, agg_send, agg_in, bm_send,
    tile_sem, x_send, x_recv, f_send, f_recv, g_send, g_recv, w_send, w_recv,
    b_send, b_recv, a_send, a_recv, m_send, m_recv,
):
    me_r, me_f = lax.axis_index("rows"), lax.axis_index("feat")
    feat_loc = x_ref.shape[0]
    blocks, slots, edge = tiles_hbm.shape[0], tiles_hbm.shape[1], tiles_hbm.shape[2]
    quarter = blocks // n_feat
    n_chip = n_rows // 2
    chip, core = me_r // 2, me_r % 2
    mate = me_r + 1 - 2 * core
    chips = [flip(chip, p, n_chip) for p in range(n_chip)]
    peers_f = [(me_f + j) % n_feat for j in range(n_feat)]
    from_f = [(me_f + n_feat - j) % n_feat for j in range(n_feat)]

    def owned(row):
        return xall.at[pl.ds(row * blocks, blocks)]

    @pl.loop(0, blocks)
    def _(i):
        pltpu.make_async_copy(tiles_hbm.at[i], tiles.at[i], tile_sem.at[i]).start()

    for i in range(blocks):
        xall[me_r * blocks + i] = x_ref[:, i * edge:(i + 1) * edge]
        gsend[i // quarter, i % quarter] = gout_ref[:, i * edge:(i + 1) * edge]

    greet([mate] + [chips[p] * 2 + core for p in range(1, n_chip)], peers_f[1:])

    x_out = []
    for p in range(1, n_chip):
        x_out.append(remote(owned(me_r), owned(me_r), x_send.at[p], x_recv.at[p], rows=chips[p] * 2 + core))
    x_out.append(remote(owned(me_r), owned(me_r), x_send.at[0], x_recv.at[0], rows=mate))
    for copy in x_out:
        copy.start()
    z_out = []
    for j in range(1, n_feat):
        z_out.append(remote(gsend.at[peers_f[j]], gall.at[me_f], g_send.at[j], g_recv.at[j], feat=peers_f[j]))
        z_out.append(remote(wt_ref, wall.at[me_f], w_send.at[j], w_recv.at[j], feat=peers_f[j]))
        z_out.append(remote(bias_ref, ball.at[me_f], b_send.at[j], b_recv.at[j], feat=peers_f[j]))
    for copy in z_out:
        copy.start()
    gall[me_f] = gsend[me_f]
    wall[me_f] = wt_ref[...]
    ball[me_f] = bias_ref[...]

    for p in range(1, n_chip):
        src = chips[p] * 2 + core
        remote(owned(src), owned(src), x_send.at[p], x_recv.at[p], rows=mate).wait_recv()
        passed = remote(owned(src), owned(src), f_send.at[p], f_recv.at[p], rows=mate)
        passed.start()
        x_out.append(passed)
    remote(owned(mate), owned(mate), x_send.at[0], x_recv.at[0], rows=mate).wait_recv()
    for p in range(1, n_chip):
        src = chips[p] * 2 + 1 - core
        remote(owned(src), owned(src), f_send.at[p], f_recv.at[p], rows=mate).wait_recv()

    agg_out = []
    for j in range(1, n_feat + 1):
        q = peers_f[j % n_feat]

        @pl.loop(0, quarter)
        def _(k):
            i = q * quarter + k
            pltpu.make_async_copy(tiles_hbm.at[i], tiles.at[i], tile_sem.at[i]).wait()
            picked = jnp.concatenate([xall[cols_ref[i, s]] for s in range(slots)], axis=1)
            vals = jnp.concatenate([tiles[i, s] for s in range(slots)], axis=1)
            agg = lax.dot_general(picked, vals, (((1,), (1,)), ((), ())), preferred_element_type=F32)
            agg_send[q, k] = agg.astype(BF16)

        if j < n_feat:
            copy = remote(agg_send.at[q], agg_in.at[me_f], a_send.at[j], a_recv.at[j], feat=q)
            copy.start()
            agg_out.append(copy)
    agg_in[me_f] = agg_send[me_f]

    for copy in z_out:
        copy.wait()
    for copy in agg_out:
        copy.wait()

    feat = n_feat * feat_loc
    gw_ref[...] = jnp.zeros_like(gw_ref)
    gb_ref[...] = jnp.zeros_like(gb_ref)
    pair = 2 if quarter % 2 == 0 else 1

    @pl.loop(0, quarter // pair)
    def _(t):
        def joined(ref):
            return jnp.concatenate([ref[:, t * pair + u].reshape(feat, edge) for u in range(pair)], axis=1)

        wt = wall[...].reshape(feat, feat)
        agg = joined(agg_in)
        preact = jnp.dot(wt, agg, preferred_element_type=F32)
        preact = preact + jnp.concatenate([ball[...].reshape(feat, edge)] * pair, axis=1)
        sigma = jax.nn.sigmoid(preact)
        act = (preact * sigma).astype(BF16)
        grad = (joined(gall).astype(F32) * sigma * (1.0 + preact * (1.0 - sigma))).astype(BF16)
        mix = lax.dot_general(wt, grad, (((0,), (0,)), ((), ())), preferred_element_type=F32).astype(BF16)
        gw_ref[...] += lax.dot_general(agg, grad, (((1,), (1,)), ((), ())), preferred_element_type=F32)
        grad32 = grad.astype(F32)
        for u in range(pair):
            cut = slice(u * edge, (u + 1) * edge)
            act_out[:, t * pair + u] = act[:, cut].reshape(n_feat, feat_loc, edge)
            bm_send[:, t * pair + u] = mix[:, cut].reshape(n_feat, feat_loc, edge)
            gb_ref[...] += grad32[:, cut]

    m_out = []
    for j in range(1, n_feat):
        copy = remote(bm_send.at[peers_f[j]], bm_in.at[me_f], m_send.at[j], m_recv.at[j], feat=peers_f[j])
        copy.start()
        m_out.append(copy)
    bm_in[me_f] = bm_send[me_f]
    for copy in x_out:
        copy.wait_send()
    for copy in m_out:
        copy.wait()


def spread_kernel(blocks, slots, edge, cols_ref, bm_ref, tiles_ref, terms_ref, acc):
    step = pl.program_id(0)

    @pl.when(step == 0)
    def _():
        acc[...] = jnp.zeros_like(acc)

    @pl.when(step < blocks)
    def _():
        vals = jnp.concatenate([tiles_ref[0, s] for s in range(slots)], axis=1)
        contrib = jnp.dot(bm_ref[step], vals, preferred_element_type=F32)
        for s in range(slots):
            col = cols_ref[step, s]
            acc[col] = acc[col] + contrib[:, s * edge:(s + 1) * edge]

    @pl.when(step >= blocks)
    def _():
        first = (step - blocks) * blocks
        terms_ref[...] = acc[pl.ds(first, blocks)].astype(BF16)


def collect_kernel(
    n_rows, n_feat, terms_ref, act_ref, gf_ref, out_ref,
    mate_in, sums, chip_in, act_in,
    t_send, t_recv, c_send, c_recv, a_send, a_recv,
):
    me_r, me_f = lax.axis_index("rows"), lax.axis_index("feat")
    blocks = terms_ref.shape[0] // n_rows
    edge = terms_ref.shape[2]
    quarter = blocks // n_feat
    n_chip = n_rows // 2
    chip, core = me_r // 2, me_r % 2
    mate = me_r + 1 - 2 * core
    chips = [flip(chip, p, n_chip) for p in range(n_chip)]
    peers_f = [(me_f + j) % n_feat for j in range(n_feat)]
    greet([mate] + [chips[p] * 2 + core for p in range(1, n_chip)], peers_f[1:])

    order = list(range(1, n_chip)) + [0]
    to_mate = {}
    for p in order:
        owner = chips[p] * 2 + 1 - core
        to_mate[p] = remote(terms_ref.at[pl.ds(owner * blocks, blocks)], mate_in.at[p],
                            t_send.at[p], t_recv.at[p], rows=mate)
        to_mate[p].start()
    act_out = []
    for j in range(1, n_feat):
        copy = remote(act_ref.at[peers_f[j]], act_in.at[me_f], a_send.at[j], a_recv.at[j], feat=peers_f[j])
        copy.start()
        act_out.append(copy)
    act_in[me_f] = act_ref[me_f]
    to_chip = {}
    for p in order:
        to_mate[p].wait_recv()
        if p:
            owner = chips[p] * 2 + core

            @pl.loop(0, blocks)
            def _(i):
                sums[p, i] = (terms_ref[owner * blocks + i].astype(F32) + mate_in[p, i].astype(F32)).astype(BF16)

            to_chip[p] = remote(sums.at[p], chip_in.at[p], c_send.at[p], c_recv.at[p], rows=owner)
            to_chip[p].start()
    for copy in act_out:
        copy.wait()
    for i in range(blocks):
        out_ref[:, i * edge:(i + 1) * edge] = act_in[i // quarter, i % quarter]
    for p in range(1, n_chip):
        to_chip[p].wait_recv()
    for i in range(blocks):
        total = terms_ref[me_r * blocks + i].astype(F32) + mate_in[0, i].astype(F32)
        for p in range(1, n_chip):
            total = total + chip_in[p, i].astype(F32)
        gf_ref[:, i * edge:(i + 1) * edge] = total
    for p in order:
        to_mate[p].wait_send()
        if p:
            to_chip[p].wait_send()


def on_device(node_feats, tile_vals, tile_cols, weight, bias_vec, grad_out):
    n_rows, n_feat = lax.axis_size("rows"), lax.axis_size("feat")
    feat_loc = node_feats.shape[0]
    blocks, slots, edge = tile_vals.shape[0], tile_vals.shape[1], tile_vals.shape[2]
    feat = feat_loc * n_feat
    quarter = blocks // n_feat
    n_chip = n_rows // 2
    vmem = pl.BlockSpec(memory_space=pltpu.VMEM)
    dma = pltpu.SemaphoreType.DMA
    flops = 2 * feat_loc * blocks * slots * edge * edge
    tile_bytes = 2 * blocks * slots * edge * edge

    parts = (n_feat, quarter, feat_loc, edge)
    bm, act, gw, gb = pl.pallas_call(
        functools.partial(forward_kernel, n_rows, n_feat),
        out_shape=(
            jax.ShapeDtypeStruct(parts, BF16),
            jax.ShapeDtypeStruct(parts, BF16),
            jax.ShapeDtypeStruct((feat, feat), F32),
            jax.ShapeDtypeStruct((feat, edge), F32),
        ),
        in_specs=[pl.BlockSpec(memory_space=pltpu.SMEM), vmem, vmem, vmem, vmem,
                  pl.BlockSpec(memory_space=pl.ANY)],
        out_specs=(vmem,) * 4,
        scratch_shapes=[
            pltpu.VMEM((n_rows * blocks, feat_loc, edge), BF16),
            pltpu.VMEM(parts, BF16),
            pltpu.VMEM(parts, BF16),
            pltpu.VMEM((n_feat, feat_loc, feat), BF16),
            pltpu.VMEM((n_feat, feat_loc, edge), F32),
            pltpu.VMEM((blocks, slots, edge, edge), BF16),
            pltpu.VMEM(parts, BF16),
            pltpu.VMEM(parts, BF16),
            pltpu.VMEM(parts, BF16),
            dma((blocks,)),
        ] + [dma((n_chip,))] * 4 + [dma((n_feat,))] * 10,
        compiler_params=pltpu.CompilerParams(
            collective_id=0, has_side_effects=True, vmem_limit_bytes=VMEM_BYTES),
        cost_estimate=pl.CostEstimate(flops=flops, bytes_accessed=tile_bytes, transcendentals=0),
        name="aggregate_and_mix",
    )(tile_cols, node_feats, grad_out, weight.T,
      jnp.broadcast_to(bias_vec[:, None], (feat_loc, edge)), tile_vals)

    gb = jnp.sum(gb, axis=1)
    grad_weight = lax.psum_scatter(gw, "feat", scatter_dimension=1, tiled=True)
    grad_bias = lax.psum_scatter(gb, "feat", scatter_dimension=0, tiled=True)
    grad_weight, grad_bias = lax.psum((grad_weight, grad_bias), "rows")

    terms = pl.pallas_call(
        functools.partial(spread_kernel, blocks, slots, edge),
        out_shape=jax.ShapeDtypeStruct((n_rows * blocks, feat_loc, edge), BF16),
        grid_spec=pltpu.PrefetchScalarGridSpec(
            num_scalar_prefetch=1,
            grid=(blocks + n_rows,),
            in_specs=[
                pl.BlockSpec((blocks, feat_loc, edge), lambda i, cols: (0, 0, 0)),
                pl.BlockSpec((1, slots, edge, edge), lambda i, cols: (jnp.minimum(i, blocks - 1), 0, 0, 0)),
            ],
            out_specs=pl.BlockSpec((blocks, feat_loc, edge), lambda i, cols: (jnp.maximum(i - blocks, 0), 0, 0)),
            scratch_shapes=[pltpu.VMEM((n_rows * blocks, feat_loc, edge), F32)],
        ),
        compiler_params=pltpu.CompilerParams(vmem_limit_bytes=VMEM_BYTES),
        cost_estimate=pl.CostEstimate(flops=flops, bytes_accessed=tile_bytes, transcendentals=0),
        name="spread_terms",
    )(tile_cols, bm.reshape(blocks, feat_loc, edge), tile_vals)

    grad_feats, activated = pl.pallas_call(
        functools.partial(collect_kernel, n_rows, n_feat),
        out_shape=(
            jax.ShapeDtypeStruct((feat_loc, blocks * edge), F32),
            jax.ShapeDtypeStruct((feat_loc, blocks * edge), BF16),
        ),
        in_specs=[vmem, vmem],
        out_specs=(vmem, vmem),
        scratch_shapes=[pltpu.VMEM((n_chip, blocks, feat_loc, edge), BF16)] * 3
        + [pltpu.VMEM(parts, BF16)]
        + [dma((n_chip,))] * 4 + [dma((n_feat,))] * 2,
        compiler_params=pltpu.CompilerParams(
            collective_id=1, has_side_effects=True, vmem_limit_bytes=VMEM_BYTES),
        cost_estimate=pl.CostEstimate(flops=1, bytes_accessed=tile_bytes // 4, transcendentals=0),
        name="collect_terms",
    )(terms, act)
    return activated, grad_feats, grad_weight, grad_bias


def solution(mesh):
    placed = (
        P("feat", "rows"),
        P("rows", None, None, None),
        P("rows", None),
        P(None, "feat"),
        P("feat"),
        P("feat", "rows"),
    )
    return jax.shard_map(
        on_device,
        mesh=mesh,
        in_specs=placed,
        out_specs=(P("feat", "rows"), P("feat", "rows"), P(None, "feat"), P("feat")),
        check_vma=False,
    )
```

time: 409 us -> 195 us (0.48)
  waiting for transfers between devices: 218 us -> 22.2 us
  Pallas kernels: 0 us -> 123 us
  other arithmetic: 78.8 us -> 0.11 us
  local copies, waits for them, and re-layouts: 49.3 us -> 12.6 us
  matrix products: 32.8 us -> 0 us
  blocking collectives: 14.1 us -> 21.7 us
    pallas_call x0 -> x3, Pallas kernels: none -> 123 us  [the longest x1 62.4 us: on_device(): pl.pallas_call(functools.partial(forward_kernel, n_rows, n_feat), out_sha...]
    all_gather x2 -> x0, waiting for transfers between devices: 85.8 us -> none  [the longest x1 46 us: on_device(): agg_all = lax.all_gather(aggregated, 'feat', axis=0, tiled=True)]
    scatter-add x1 -> x0, other arithmetic: 78.1 us -> none  [on_device(): terms = jnp.zeros((feat_loc, row_devs * own_blocks, tile_edge), jnp.float...]
    reduce_scatter x1 -> x0, waiting for transfers between devices: 57.7 us -> none  [on_device(): lax.psum_scatter(terms.reshape(feat_loc, -1), 'rows', scatter_dimension=1...]
    unnamed x6 -> x3, waiting for transfers between devices: 74.7 us -> 22.2 us
    dot_general x5 -> x0, matrix products: 32.8 us -> none  [the longest x1 14 us: on_device(): jnp.einsum('fia,isab->fisb', back_mix.reshape(feat_loc, own_blocks, tile_...]
    gather x1 -> x0, local copies, waits for them, and re-layouts: 21.8 us -> none  [on_device(): picked = jnp.take(whole.reshape(feat_loc, -1, tile_edge), flat_cols, axis=1)]
    reshape x3 -> x0, local copies, waits for them, and re-layouts: 12.6 us -> none  [the longest x1 7.15 us: on_device(): terms.reshape(feat_loc, -1)]
  transfers between devices with their start and end apart: 5 -> 2, of which waited for: 4 -> 1; matrix products, arithmetic and copies ran while one was open for 27% -> 0% of each run, Pallas kernels for 0% -> 31%
where the time goes in v1:
time: 195 us; the launch traced here: 194 us
  Pallas kernels  123 us (63%)
  waiting for transfers between devices  22.2 us (11%)
  blocking collectives  21.7 us (11%)
  between operations  14.7 us (8%)
  local copies, waits for them, and re-layouts  12.6 us (6%)
    pallas_call x1, Pallas kernels, on_device(): pl.pallas_call(functools.partial(forward_kernel, n_rows, n_feat), out_sha...  62.4 us
    pallas_call x1, Pallas kernels, on_device(): pl.pallas_call(functools.partial(collect_kernel, n_rows, n_feat), out_sha...  33.2 us
    pallas_call x1, Pallas kernels, on_device(): pl.pallas_call(functools.partial(spread_kernel, blocks, slots, edge), out...  27.3 us
    unnamed x3, waiting for transfers between devices  22.2 us
    psum x1, blocking collectives, on_device(): grad_weight, grad_bias = lax.psum((grad_weight, grad_bias), 'rows')  12.4 us
    unnamed x12, local copies, waits for them, and re-layouts  11.2 us
    unnamed x1, blocking collectives  9.32 us
  transfers between devices with their start and end apart: 2, of which 1 were waited for; matrix products, arithmetic and copies ran while one was open for 0% of the time, Pallas kernels for 31%

profile of v1, /device:TPU:0, one launch (start us, length us, event | category | flops | bytes accessed | tf_op | source)
XLA Modules:
  0.0 194.2 jit_solution(1251463133768020593)
XLA Ops:
  7.2 0.0 reduce-scatter.4.cloned.1.call-start
  7.2 1.4 copy.14.cols_ref
  8.6 1.3 broadcast_in_dim.2.bias_ref
  9.9 62.4 %aggregate_and_mix.1 = (bf16[4,8,64,128]{3,2,1,0:T(8,128)(2,1)}, bf16[4,8,64,128]{3,2,1,0:T(8,128)(2,1)}, f32[256,256]{1,0:T(8,128)}, f32[256,128]{1,0:T(8,128)}) custom-call(s32[32,16]{1,0:T(8,128)} %copy.14.cols_ref, bf16[64,4096]{1,0:T(8,128)(2,1)} %x_ref.1, bf16[64,4096]{1,0:T(8,128)(2,1)} %gout_ref.1, bf16[64,256]{1,0:T(8,128)(2,1)} %bitcast.8, ...), custom_call_target="tpu_custom_call" | custom-call | flops 1073741824 | bytes 16777216 | tf_op jit(solution)/shard_map/aggregate_and_mix/pallas_call | solution.py:255
  72.3 0.0 copy-start.1
  72.3 0.0 copy-start
  72.4 1.8 copy.16
  74.2 0.0 reduce-scatter.4.cloned.1.call-update
  74.2 0.0 all-reduce.3.cloned.1.call-start
  74.3 22.1 %reduce-scatter.4.cloned.1.call-done = f32[64,256]{1,0:T(8,128)} async-done(((f32[256,256]{1,0:T(8,128)}), f32[64,256]{1,0:T(8,128)}) %reduce-scatter.4.cloned.1.call-update) | async-done | bytes 65552
  96.4 1.6 copy.17
  98.0 0.0 all-reduce.3.cloned.1.call-update
  98.0 27.3 %spread_terms.1.terms_ref = bf16[256,64,128]{2,1,0:T(8,128)(2,1)} custom-call(s32[32,16]{1,0:T(8,128)} %copy.14.cols_ref, bf16[32,64,128]{2,1,0:T(8,128)(2,1)} %bitcast.6, bf16[32,16,128,128]{3,2,1,0:T(8,128)(2,1)} %tiles_ref.1), custom_call_target="tpu_custom_call" | custom-call | flops 1073741824 | bytes 16777216 | tf_op jit(solution)/shard_map/spread_terms/pallas_call | solution.py:290
  125.3 33.2 %collect_terms.1 = (f32[64,4096]{1,0:T(8,128)}, bf16[64,4096]{1,0:T(8,128)(2,1)}) custom-call(bf16[256,64,128]{2,1,0:T(8,128)(2,1)} %spread_terms.1.terms_ref, bf16[4,8,64,128]{3,2,1,0:T(8,128)(2,1)} %get-tuple-element.11.act_ref), custom_call_target="tpu_custom_call" | custom-call | flops 1 | bytes 4194304 | tf_op jit(solution)/shard_map/collect_terms/pallas_call | solution.py:308
  158.5 0.0 copy-done.1
  158.5 0.6 dynamic-slice
  159.8 0.0 copy-done
  159.8 0.1 reduce_sum.9
  159.9 9.3 %all-reduce = f32[256]{0:T(256)S(1)} all-reduce(f32[256]{0:T(256)S(1)} %reduce_sum.9), channel_id=3, replica_groups=mesh['rows'=8,'feat'=4] {'feat'}, use_global_device_ids=true, to_apply=%region_3.0.clone | all-reduce | flops 256 | bytes 2048
  169.2 0.1 dynamic-slice.1
  169.3 12.4 %psum.15 = f32[64]{0:T(128)} all-reduce(f32[64]{0:T(128)S(1)} %dynamic-slice.1), channel_id=1, replica_groups=mesh['rows'=8,'feat'=4] {'rows'}, use_global_device_ids=true, to_apply=%region_4.0 | all-reduce | flops 64 | bytes 512 | tf_op jit(solution)/shard_map/psum | solution.py:288
  181.6 0.0 all-reduce.3.cloned.1.call-done
  181.6 1.6 copy.15
  183.3 1.9 copy.21
  185.1 2.3 %copy.22 = f32[64,4096]{1,0:T(8,128)} copy(f32[64,4096]{1,0:T(8,128)} %get-tuple-element.29) | data formatting | bytes 2097152
Async XLA Ops:
  7.2 89.2 %reduce-scatter.4.cloned.1.call-start = ((), (), s32[]{:S(2)}) async-start(), calls=%async_computation.2 | async-start | bytes 327680
  72.3 86.2 %copy-start.1 = (u32[32]{0:T(128)S(1)}, u32[32]{0:T(128)}, u32[]{:S(2)}) copy-start(u32[32]{0:T(128)} %constant.4) | copy-start | bytes 388
  72.3 87.4 %copy-start = (f32[256,128]{1,0:T(8,128)S(1)}, f32[256,128]{1,0:T(8,128)}, u32[]{:S(2)}) copy-start(f32[256,128]{1,0:T(8,128)} %get-tuple-element.15) | copy-start | bytes 393220
  74.2 107.4 %all-reduce.3.cloned.1.call-start = ((), (), s32[]{:S(2)}) async-start(), calls=%async_computation.1 | async-start | bytes 262144 | tf_op jit(solution)/shard_map/psum | solution.py:288
Sparse Core Ops, SparseCore 0:
  74.3 22.0 reduce-scatter.3
  100.3 59.4 all-reduce.2

commit v2 on v1

--- a/solution.py
+++ b/solution.py
@@ -41,7 +41,7 @@
 def forward_kernel(
     n_rows, n_feat,
     cols_ref, x_ref, gout_ref, wt_ref, bias_ref, tiles_hbm,
-    bm_in, act_out, gw_ref, gb_ref,
+    bm_in, act_out, gw_ref,
     xall, gsend, gall, wall, ball, tiles, agg_send, agg_in, bm_send,
     tile_sem, x_send, x_recv, f_send, f_recv, g_send, g_recv, w_send, w_recv,
     b_send, b_recv, a_send, a_recv, m_send, m_recv,
@@ -98,18 +98,22 @@
         src = chips[p] * 2 + 1 - core
         remote(owned(src), owned(src), f_send.at[p], f_recv.at[p], rows=mate).wait_recv()
 
+    group = 4 if quarter % 4 == 0 else 1
     agg_out = []
     for j in range(1, n_feat + 1):
         q = peers_f[j % n_feat]
 
-        @pl.loop(0, quarter)
-        def _(k):
-            i = q * quarter + k
-            pltpu.make_async_copy(tiles_hbm.at[i], tiles.at[i], tile_sem.at[i]).wait()
-            picked = jnp.concatenate([xall[cols_ref[i, s]] for s in range(slots)], axis=1)
-            vals = jnp.concatenate([tiles[i, s] for s in range(slots)], axis=1)
-            agg = lax.dot_general(picked, vals, (((1,), (1,)), ((), ())), preferred_element_type=F32)
-            agg_send[q, k] = agg.astype(BF16)
+        @pl.loop(0, quarter // group)
+        def _(g):
+            first = q * quarter + g * group
+            for u in range(group):
+                pltpu.make_async_copy(tiles_hbm.at[first + u], tiles.at[first + u], tile_sem.at[first + u]).wait()
+            for u in range(group):
+                i = first + u
+                picked = jnp.concatenate([xall[cols_ref[s, i]] for s in range(slots)], axis=1)
+                vals = jnp.concatenate([tiles[i, s] for s in range(slots)], axis=1)
+                agg = lax.dot_general(picked, vals, (((1,), (1,)), ((), ())), preferred_element_type=F32)
+                agg_send[q, g * group + u] = agg.astype(BF16)
 
         if j < n_feat:
             copy = remote(agg_send.at[q], agg_in.at[me_f], a_send.at[j], a_recv.at[j], feat=q)
@@ -124,8 +128,12 @@
 
     feat = n_feat * feat_loc
     gw_ref[...] = jnp.zeros_like(gw_ref)
-    gb_ref[...] = jnp.zeros_like(gb_ref)
     pair = 2 if quarter % 2 == 0 else 1
+
+    def mix_copy(j, t):
+        part = pl.ds(t * pair, pair)
+        return remote(bm_send.at[peers_f[j], part], bm_in.at[me_f, part],
+                      m_send.at[j, t], m_recv.at[j, t], feat=peers_f[j])
 
     @pl.loop(0, quarter // pair)
     def _(t):
@@ -140,51 +148,55 @@
         act = (preact * sigma).astype(BF16)
         grad = (joined(gall).astype(F32) * sigma * (1.0 + preact * (1.0 - sigma))).astype(BF16)
         mix = lax.dot_general(wt, grad, (((0,), (0,)), ((), ())), preferred_element_type=F32).astype(BF16)
-        gw_ref[...] += lax.dot_general(agg, grad, (((1,), (1,)), ((), ())), preferred_element_type=F32)
+        part = lax.dot_general(grad, agg, (((1,), (1,)), ((), ())), preferred_element_type=F32)
+        gw_ref[:, :, :feat] += part.reshape(n_feat, feat_loc, feat)
         grad32 = grad.astype(F32)
         for u in range(pair):
             cut = slice(u * edge, (u + 1) * edge)
             act_out[:, t * pair + u] = act[:, cut].reshape(n_feat, feat_loc, edge)
             bm_send[:, t * pair + u] = mix[:, cut].reshape(n_feat, feat_loc, edge)
-            gb_ref[...] += grad32[:, cut]
-
-    m_out = []
-    for j in range(1, n_feat):
-        copy = remote(bm_send.at[peers_f[j]], bm_in.at[me_f], m_send.at[j], m_recv.at[j], feat=peers_f[j])
-        copy.start()
-        m_out.append(copy)
+            gw_ref[:, :, feat:] += grad32[:, cut].reshape(n_feat, feat_loc, edge)
+        for j in range(1, n_feat):
+            mix_copy(j, t).start()
+
     bm_in[me_f] = bm_send[me_f]
     for copy in x_out:
         copy.wait_send()
-    for copy in m_out:
-        copy.wait()
-
-
-def spread_kernel(blocks, slots, edge, cols_ref, bm_ref, tiles_ref, terms_ref, acc):
+    @pl.loop(0, quarter // pair)
+    def _(t):
+        for j in range(1, n_feat):
+            mix_copy(j, t).wait()
+
+
+def spread_kernel(blocks, slots, edge, group, cols_ref, bm_ref, tiles_ref, terms_ref, acc):
     step = pl.program_id(0)
+    steps = blocks // group
 
     @pl.when(step == 0)
     def _():
         acc[...] = jnp.zeros_like(acc)
 
-    @pl.when(step < blocks)
+    @pl.when(step < steps)
     def _():
-        vals = jnp.concatenate([tiles_ref[0, s] for s in range(slots)], axis=1)
-        contrib = jnp.dot(bm_ref[step], vals, preferred_element_type=F32)
-        for s in range(slots):
-            col = cols_ref[step, s]
-            acc[col] = acc[col] + contrib[:, s * edge:(s + 1) * edge]
-
-    @pl.when(step >= blocks)
+        for u in range(group):
+            i = step * group + u
+            vals = jnp.concatenate([tiles_ref[u, s] for s in range(slots)], axis=1)
+            contrib = jnp.dot(bm_ref[i], vals, preferred_element_type=F32)
+            for s in range(slots):
+                col = cols_ref[s, i]
+                acc[col] = acc[col] + contrib[:, s * edge:(s + 1) * edge]
+
+    @pl.when(step >= steps)
     def _():
-        first = (step - blocks) * blocks
-        terms_ref[...] = acc[pl.ds(first, blocks)].astype(BF16)
+        count = terms_ref.shape[0]
+        first = (step - steps) * count
+        terms_ref[...] = acc[pl.ds(first, count)].astype(BF16)
 
 
 def collect_kernel(
-    n_rows, n_feat, terms_ref, act_ref, gf_ref, out_ref,
-    mate_in, sums, chip_in, act_in,
-    t_send, t_recv, c_send, c_recv, a_send, a_recv,
+    n_rows, n_feat, terms_ref, act_ref, gw_ref, gf_ref, out_ref, gw_out,
+    mate_in, sums, chip_in, act_in, gw_in, gw_sum, gw_mate, gw_chip, gw_full,
+    t_send, t_recv, c_send, c_recv, h_send, h_recv, a_send, a_recv, g_send, g_recv, e_send, e_recv,
 ):
     me_r, me_f = lax.axis_index("rows"), lax.axis_index("feat")
     blocks = terms_ref.shape[0] // n_rows
@@ -197,19 +209,25 @@
     peers_f = [(me_f + j) % n_feat for j in range(n_feat)]
     greet([mate] + [chips[p] * 2 + core for p in range(1, n_chip)], peers_f[1:])
 
-    order = list(range(1, n_chip)) + [0]
+    order = list(range(n_chip - 1, -1, -1))
     to_mate = {}
     for p in order:
         owner = chips[p] * 2 + 1 - core
         to_mate[p] = remote(terms_ref.at[pl.ds(owner * blocks, blocks)], mate_in.at[p],
                             t_send.at[p], t_recv.at[p], rows=mate)
         to_mate[p].start()
+    gw_feat = []
+    for j in range(1, n_feat):
+        copy = remote(gw_ref.at[peers_f[j]], gw_in.at[me_f], g_send.at[j], g_recv.at[j], feat=peers_f[j])
+        copy.start()
+        gw_feat.append(copy)
     act_out = []
     for j in range(1, n_feat):
         copy = remote(act_ref.at[peers_f[j]], act_in.at[me_f], a_send.at[j], a_recv.at[j], feat=peers_f[j])
         copy.start()
         act_out.append(copy)
     act_in[me_f] = act_ref[me_f]
+    gw_in[me_f] = gw_ref[me_f]
     to_chip = {}
     for p in order:
         to_mate[p].wait_recv()
@@ -222,10 +240,33 @@
 
             to_chip[p] = remote(sums.at[p], chip_in.at[p], c_send.at[p], c_recv.at[p], rows=owner)
             to_chip[p].start()
+    half = gw_in.shape[1] // 2
+    for copy in gw_feat:
+        copy.wait()
+    gw_sum[...] = sum(gw_in[f] for f in range(n_feat))
+    mine, other = pl.ds(core * half, half), pl.ds((1 - core) * half, half)
+    swap = remote(gw_sum.at[other], gw_mate, e_send.at[0], e_recv.at[0], rows=mate)
+    swap.start()
+    swap.wait()
+    gw_chip[chip] = gw_sum[mine] + gw_mate[...]
+    gw_chips = []
+    for p in range(1, n_chip):
+        copy = remote(gw_chip.at[chip], gw_chip.at[chip], h_send.at[p], h_recv.at[p], rows=chips[p] * 2 + core)
+        copy.start()
+        gw_chips.append(copy)
     for copy in act_out:
         copy.wait()
     for i in range(blocks):
         out_ref[:, i * edge:(i + 1) * edge] = act_in[i // quarter, i % quarter]
+    for p in range(1, n_chip):
+        gw_chips[p - 1].wait_send()
+        remote(gw_chip.at[chips[p]], gw_chip.at[chips[p]], h_send.at[p], h_recv.at[p], rows=mate).wait_recv()
+    total_half = gw_chip[0]
+    for c in range(1, n_chip):
+        total_half = total_half + gw_chip[c]
+    gw_full[mine] = total_half
+    back = remote(gw_full.at[mine], gw_full.at[mine], e_send.at[1], e_recv.at[1], rows=mate)
+    back.start()
     for p in range(1, n_chip):
         to_chip[p].wait_recv()
     for i in range(blocks):
@@ -237,6 +278,9 @@
         to_mate[p].wait_send()
         if p:
             to_chip[p].wait_send()
+    back.wait_send()
+    remote(gw_full.at[other], gw_full.at[other], e_send.at[1], e_recv.at[1], rows=mate).wait_recv()
+    gw_out[...] = gw_full[...]
 
 
 def on_device(node_feats, tile_vals, tile_cols, weight, bias_vec, grad_out):
@@ -252,17 +296,19 @@
     tile_bytes = 2 * blocks * slots * edge * edge
 
     parts = (n_feat, quarter, feat_loc, edge)
-    bm, act, gw, gb = pl.pallas_call(
+    cols = tile_cols.T
+    wide = feat + edge
+    pairs = quarter // 2 if quarter % 2 == 0 else quarter
+    bm, act, gw = pl.pallas_call(
         functools.partial(forward_kernel, n_rows, n_feat),
         out_shape=(
             jax.ShapeDtypeStruct(parts, BF16),
             jax.ShapeDtypeStruct(parts, BF16),
-            jax.ShapeDtypeStruct((feat, feat), F32),
-            jax.ShapeDtypeStruct((feat, edge), F32),
+            jax.ShapeDtypeStruct((n_feat, feat_loc, wide), F32),
         ),
         in_specs=[pl.BlockSpec(memory_space=pltpu.SMEM), vmem, vmem, vmem, vmem,
                   pl.BlockSpec(memory_space=pl.ANY)],
-        out_specs=(vmem,) * 4,
+        out_specs=(vmem,) * 3,
         scratch_shapes=[
             pltpu.VMEM((n_rows * blocks, feat_loc, edge), BF16),
             pltpu.VMEM(parts, BF16),
@@ -274,53 +320,60 @@
             pltpu.VMEM(parts, BF16),
             pltpu.VMEM(parts, BF16),
             dma((blocks,)),
-        ] + [dma((n_chip,))] * 4 + [dma((n_feat,))] * 10,
+        ] + [dma((n_chip,))] * 4 + [dma((n_feat,))] * 8 + [dma((n_feat, pairs))] * 2,
         compiler_params=pltpu.CompilerParams(
             collective_id=0, has_side_effects=True, vmem_limit_bytes=VMEM_BYTES),
         cost_estimate=pl.CostEstimate(flops=flops, bytes_accessed=tile_bytes, transcendentals=0),
         name="aggregate_and_mix",
-    )(tile_cols, node_feats, grad_out, weight.T,
+    )(cols, node_feats, grad_out, weight.T,
       jnp.broadcast_to(bias_vec[:, None], (feat_loc, edge)), tile_vals)
 
-    gb = jnp.sum(gb, axis=1)
-    grad_weight = lax.psum_scatter(gw, "feat", scatter_dimension=1, tiled=True)
-    grad_bias = lax.psum_scatter(gb, "feat", scatter_dimension=0, tiled=True)
-    grad_weight, grad_bias = lax.psum((grad_weight, grad_bias), "rows")
-
+    group = 4 if blocks % 4 == 0 else 1
+    steps = blocks // group
+    owners = 4 if n_rows % 4 == 0 else 1
     terms = pl.pallas_call(
-        functools.partial(spread_kernel, blocks, slots, edge),
+        functools.partial(spread_kernel, blocks, slots, edge, group),
         out_shape=jax.ShapeDtypeStruct((n_rows * blocks, feat_loc, edge), BF16),
         grid_spec=pltpu.PrefetchScalarGridSpec(
             num_scalar_prefetch=1,
-            grid=(blocks + n_rows,),
+            grid=(steps + n_rows // owners,),
             in_specs=[
                 pl.BlockSpec((blocks, feat_loc, edge), lambda i, cols: (0, 0, 0)),
-                pl.BlockSpec((1, slots, edge, edge), lambda i, cols: (jnp.minimum(i, blocks - 1), 0, 0, 0)),
+                pl.BlockSpec((group, slots, edge, edge), lambda i, cols: (jnp.minimum(i, steps - 1), 0, 0, 0)),
             ],
-            out_specs=pl.BlockSpec((blocks, feat_loc, edge), lambda i, cols: (jnp.maximum(i - blocks, 0), 0, 0)),
+            out_specs=pl.BlockSpec((owners * blocks, feat_loc, edge), lambda i, cols: (jnp.maximum(i - steps, 0), 0, 0)),
             scratch_shapes=[pltpu.VMEM((n_rows * blocks, feat_loc, edge), F32)],
         ),
         compiler_params=pltpu.CompilerParams(vmem_limit_bytes=VMEM_BYTES),
         cost_estimate=pl.CostEstimate(flops=flops, bytes_accessed=tile_bytes, transcendentals=0),
         name="spread_terms",
-    )(tile_cols, bm.reshape(blocks, feat_loc, edge), tile_vals)
-
-    grad_feats, activated = pl.pallas_call(
+    )(cols, bm.reshape(blocks, feat_loc, edge), tile_vals)
+
+    grad_feats, activated, gw = pl.pallas_call(
         functools.partial(collect_kernel, n_rows, n_feat),
         out_shape=(
             jax.ShapeDtypeStruct((feat_loc, blocks * edge), F32),
             jax.ShapeDtypeStruct((feat_loc, blocks * edge), BF16),
+            jax.ShapeDtypeStruct((feat_loc, wide), F32),
         ),
-        in_specs=[vmem, vmem],
-        out_specs=(vmem, vmem),
+        in_specs=[vmem] * 3,
+        out_specs=(vmem,) * 3,
         scratch_shapes=[pltpu.VMEM((n_chip, blocks, feat_loc, edge), BF16)] * 3
-        + [pltpu.VMEM(parts, BF16)]
-        + [dma((n_chip,))] * 4 + [dma((n_feat,))] * 2,
+        + [
+            pltpu.VMEM(parts, BF16),
+            pltpu.VMEM((n_feat, feat_loc, wide), F32),
+            pltpu.VMEM((feat_loc, wide), F32),
+            pltpu.VMEM((feat_loc // 2, wide), F32),
+            pltpu.VMEM((n_chip, feat_loc // 2, wide), F32),
+            pltpu.VMEM((feat_loc, wide), F32),
+        ]
+        + [dma((n_chip,))] * 6 + [dma((n_feat,))] * 4 + [dma((2,))] * 2,
         compiler_params=pltpu.CompilerParams(
             collective_id=1, has_side_effects=True, vmem_limit_bytes=VMEM_BYTES),
         cost_estimate=pl.CostEstimate(flops=1, bytes_accessed=tile_bytes // 4, transcendentals=0),
         name="collect_terms",
-    )(terms, act)
+    )(terms, act, gw)
+    grad_weight, grad_bias = gw[:, :feat].T, jnp.sum(gw[:, feat:], axis=1)
     return activated, grad_feats, grad_weight, grad_bias
 
 

time: 195 us -> 121 us (0.62)
  waiting for transfers between devices: 22.2 us -> 0 us
  blocking collectives: 21.7 us -> 0 us
  between operations: 14.7 us -> 0.65 us
  Pallas kernels: 123 us -> 112 us
  local copies, waits for them, and re-layouts: 12.6 us -> 6.95 us
    unnamed x3 -> x0, waiting for transfers between devices: 22.2 us -> none
    pallas_call x1, Pallas kernels: 27.3 us -> 13.5 us  [on_device(): pl.pallas_call(functools.partial(spread_kernel, blocks, slots, edge, grou...]
    psum x1 -> x0, blocking collectives: 12.4 us -> none  [on_device(): grad_weight, grad_bias = lax.psum((grad_weight, grad_bias), 'rows')]
    unnamed x1 -> x0, blocking collectives: 9.32 us -> none
    unnamed x12 -> x2, local copies, waits for them, and re-layouts: 11.2 us -> 4.14 us
    pallas_call x1, Pallas kernels: 33.2 us -> 36.1 us  [on_device(): pl.pallas_call(functools.partial(collect_kernel, n_rows, n_feat), out_sha...]
  transfers between devices with their start and end apart: 2 -> 0, of which waited for: 1 -> 0; matrix products, arithmetic and copies ran while one was open for 0% -> 0% of each run, Pallas kernels for 31% -> 0%
where the time goes in v2:
time: 121 us
  Pallas kernels  112 us (93%)
  local copies, waits for them, and re-layouts  6.95 us (6%)
  other arithmetic  1.38 us (1%)
    pallas_call x1, Pallas kernels, on_device(): pl.pallas_call(functools.partial(forward_kernel, n_rows, n_feat), out_sha...  62.4 us
    pallas_call x1, Pallas kernels, on_device(): pl.pallas_call(functools.partial(collect_kernel, n_rows, n_feat), out_sha...  36.1 us
    pallas_call x1, Pallas kernels, on_device(): pl.pallas_call(functools.partial(spread_kernel, blocks, slots, edge, grou...  13.5 us
    unnamed x2, local copies, waits for them, and re-layouts  4.14 us

profile of v2, /device:TPU:0, one launch (start us, length us, event | category | flops | bytes accessed | tf_op | source)
XLA Modules:
  0.0 121.0 jit_solution(7475743060486930397)
XLA Ops:
  0.6 1.3 %broadcast_in_dim.2.bias_ref = f32[64,128]{1,0:T(8,128)} broadcast(f32[64]{0:T(128)} %param.10), dimensions={0} | broadcast | bytes 33024 | tf_op jit(solution)/shard_map/broadcast_in_dim | solution.py:329
  2.0 62.4 %aggregate_and_mix.1 = (bf16[4,8,64,128]{3,2,1,0:T(8,128)(2,1)}, bf16[4,8,64,128]{3,2,1,0:T(8,128)(2,1)}, f32[4,64,384]{2,1,0:T(8,128)}) custom-call(s32[16,32]{1,0:T(8,128)} %bitcast.6, bf16[64,4096]{1,0:T(8,128)(2,1)} %x_ref.1, bf16[64,4096]{1,0:T(8,128)(2,1)} %gout_ref.1, bf16[64,256]{1,0:T(8,128)(2,1)} %bitcast.8, f32[64,128]{1,0:T(8,128)} %broadcast_in_dim.2.bias_ref, ...), custom_call_target="tpu_custom_call" | custom-call | flops 1073741824 | bytes 16777216 | tf_op jit(solution)/shard_map/aggregate_and_mix/pallas_call | solution.py:302
  64.3 13.5 %spread_terms.1.terms_ref = bf16[256,64,128]{2,1,0:T(8,128)(2,1)} custom-call(s32[16,32]{1,0:T(8,128)} %bitcast.7, bf16[32,64,128]{2,1,0:T(8,128)(2,1)} %bitcast.5, bf16[32,16,128,128]{3,2,1,0:T(8,128)(2,1)} %tiles_ref.1), custom_call_target="tpu_custom_call" | custom-call | flops 1073741824 | bytes 16777216 | tf_op jit(solution)/shard_map/spread_terms/pallas_call | solution.py:334
  77.9 36.1 %collect_terms.1 = (f32[64,4096]{1,0:T(8,128)}, bf16[64,4096]{1,0:T(8,128)(2,1)}, f32[64,384]{1,0:T(8,128)}) custom-call(bf16[256,64,128]{2,1,0:T(8,128)(2,1)} %spread_terms.1.terms_ref, bf16[4,8,64,128]{3,2,1,0:T(8,128)(2,1)} %get-tuple-element.11.act_ref, f32[4,64,384]{2,1,0:T(8,128)} %get-tuple-element.12.gw_ref), custom_call_target="tpu_custom_call" | custom-call | flops 1 | bytes 4194304 | tf_op jit(solution)/shard_map/collect_terms/pallas_call | solution.py:352
  114.0 1.4 %slice_reduce_fusion = f32[64]{0:T(128)} fusion(f32[64,384]{1,0:T(8,128)} %get-tuple-element.15), kind=kLoop, calls=%fused_computation.1 | loop fusion | flops 8128 | bytes 33024 | tf_op jit(solution)/shard_map/reduce_sum | solution.py:376
  115.4 1.5 %slice_bitcast_fusion = f32[256,64]{0,1:T(8,128)} fusion(f32[64,384]{1,0:T(8,128)} %get-tuple-element.15), kind=kLoop, calls=%fused_computation | loop fusion | bytes 131072 | tf_op jit(solution)/shard_map/transpose | solution.py:376
  116.9 1.9 %copy.12 = bf16[64,4096]{1,0:T(8,128)(2,1)} copy(bf16[64,4096]{1,0:T(8,128)(2,1)} %get-tuple-element.20) | data formatting | bytes 1048576
  118.7 2.3 %copy.13 = f32[64,4096]{1,0:T(8,128)} copy(f32[64,4096]{1,0:T(8,128)} %get-tuple-element.21) | data formatting | bytes 2097152

commit v3 on v2

--- a/solution.py
+++ b/solution.py
@@ -57,9 +57,6 @@
     peers_f = [(me_f + j) % n_feat for j in range(n_feat)]
     from_f = [(me_f + n_feat - j) % n_feat for j in range(n_feat)]
 
-    def owned(row):
-        return xall.at[pl.ds(row * blocks, blocks)]
-
     @pl.loop(0, blocks)
     def _(i):
         pltpu.make_async_copy(tiles_hbm.at[i], tiles.at[i], tile_sem.at[i]).start()
@@ -70,10 +67,22 @@
 
     greet([mate] + [chips[p] * 2 + core for p in range(1, n_chip)], peers_f[1:])
 
-    x_out = []
-    for p in range(1, n_chip):
-        x_out.append(remote(owned(me_r), owned(me_r), x_send.at[p], x_recv.at[p], rows=chips[p] * 2 + core))
-    x_out.append(remote(owned(me_r), owned(me_r), x_send.at[0], x_recv.at[0], rows=mate))
+    half = blocks // 2
+    relayed = n_chip == 4
+
+    def owned(row, h):
+        return xall.at[pl.ds(row * blocks + h * half, half)]
+
+    def hand(origin, p, h, target):
+        return remote(owned(origin, h), owned(origin, h), x_send.at[p, h], x_recv.at[p, h], rows=target)
+
+    near = [chips[p] * 2 + core for p in range(n_chip)]
+    if relayed:
+        first = [(1, 0), (2, 1), (1, 1), (2, 0)]
+        arrivals = first + [(3, 0), (3, 1)]
+    else:
+        first = arrivals = [(p, h) for p in range(1, n_chip) for h in (0, 1)]
+    x_out = [hand(me_r, p, h, near[p]) for p, h in first] + [hand(me_r, 0, h, mate) for h in (0, 1)]
     for copy in x_out:
         copy.start()
     z_out = []
@@ -87,16 +96,21 @@
     wall[me_f] = wt_ref[...]
     ball[me_f] = bias_ref[...]
 
-    for p in range(1, n_chip):
-        src = chips[p] * 2 + core
-        remote(owned(src), owned(src), x_send.at[p], x_recv.at[p], rows=mate).wait_recv()
-        passed = remote(owned(src), owned(src), f_send.at[p], f_recv.at[p], rows=mate)
+    for p, h in arrivals:
+        src = near[p]
+        hand(src, p, h, mate).wait_recv()
+        if relayed and (p, h) in ((1, 0), (2, 1)):
+            onward = hand(src, 3, h, near[3 - p])
+            onward.start()
+            x_out.append(onward)
+        passed = remote(owned(src, h), owned(src, h), f_send.at[p, h], f_recv.at[p, h], rows=mate)
         passed.start()
         x_out.append(passed)
-    remote(owned(mate), owned(mate), x_send.at[0], x_recv.at[0], rows=mate).wait_recv()
-    for p in range(1, n_chip):
+    for h in (0, 1):
+        hand(mate, 0, h, mate).wait_recv()
+    for p, h in arrivals:
         src = chips[p] * 2 + 1 - core
-        remote(owned(src), owned(src), f_send.at[p], f_recv.at[p], rows=mate).wait_recv()
+        remote(owned(src, h), owned(src, h), f_send.at[p, h], f_recv.at[p, h], rows=mate).wait_recv()
 
     group = 4 if quarter % 4 == 0 else 1
     agg_out = []
@@ -194,8 +208,8 @@
 
 
 def collect_kernel(
-    n_rows, n_feat, terms_ref, act_ref, gw_ref, gf_ref, out_ref, gw_out,
-    mate_in, sums, chip_in, act_in, gw_in, gw_sum, gw_mate, gw_chip, gw_full,
+    n_rows, n_feat, terms_ref, act_ref, gw_ref, gf_ref, out_ref, gw_out, gb_out,
+    mate_in, sums, chip_in, diag_in, act_in, gw_in, gw_sum, gw_mate, gw_chip, gw_full,
     t_send, t_recv, c_send, c_recv, h_send, h_recv, a_send, a_recv, g_send, g_recv, e_send, e_recv,
 ):
     me_r, me_f = lax.axis_index("rows"), lax.axis_index("feat")
@@ -209,7 +223,8 @@
     peers_f = [(me_f + j) % n_feat for j in range(n_feat)]
     greet([mate] + [chips[p] * 2 + core for p in range(1, n_chip)], peers_f[1:])
 
-    order = list(range(n_chip - 1, -1, -1))
+    relayed = n_chip == 4
+    order = [3, 1, 2, 0] if relayed else list(range(n_chip - 1, -1, -1))
     to_mate = {}
     for p in order:
         owner = chips[p] * 2 + 1 - core
@@ -228,18 +243,52 @@
         act_out.append(copy)
     act_in[me_f] = act_ref[me_f]
     gw_in[me_f] = gw_ref[me_f]
-    to_chip = {}
-    for p in order:
-        to_mate[p].wait_recv()
-        if p:
-            owner = chips[p] * 2 + core
-
-            @pl.loop(0, blocks)
-            def _(i):
-                sums[p, i] = (terms_ref[owner * blocks + i].astype(F32) + mate_in[p, i].astype(F32)).astype(BF16)
-
-            to_chip[p] = remote(sums.at[p], chip_in.at[p], c_send.at[p], c_recv.at[p], rows=owner)
-            to_chip[p].start()
+    span = blocks // 2
+    near = [chips[p] * 2 + core for p in range(n_chip)]
+    sent = []
+
+    def summed(p, h, extra=None):
+        @pl.loop(0, span)
+        def _(i):
+            at = h * span + i
+            total = terms_ref[near[p] * blocks + at].astype(F32) + mate_in[p, at].astype(F32)
+            if extra is not None:
+                total = total + extra[i].astype(F32)
+            sums[p, at] = total.astype(BF16)
+
+    def ship(p, h, target, landing, slot):
+        copy = remote(sums.at[p, pl.ds(h * span, span)], landing, c_send.at[p, h], c_recv.at[slot, h], rows=near[target])
+        copy.start()
+        sent.append(copy)
+
+    def landed(slot, h, landing):
+        remote(landing, landing, c_send.at[slot, h], c_recv.at[slot, h], rows=mate).wait_recv()
+
+    def chip_half(p, h):
+        return chip_in.at[p, pl.ds(h * span, span)]
+
+    if relayed:
+        to_mate[3].wait_recv()
+        for h in (0, 1):
+            summed(3, h)
+            ship(3, h, 1 + h, diag_in.at[h], 3)
+        for h in (0, 1):
+            to_mate[1 + h].wait_recv()
+            summed(1 + h, h)
+            ship(1 + h, h, 1 + h, chip_half(1 + h, h), 1 + h)
+        for h in (0, 1):
+            landed(3, h, diag_in.at[h])
+            summed(2 - h, h, diag_in.at[h])
+            ship(2 - h, h, 2 - h, chip_half(2 - h, h), 2 - h)
+        to_mate[0].wait_recv()
+    else:
+        for p in order:
+            to_mate[p].wait_recv()
+            if p:
+                for h in (0, 1):
+                    summed(p, h)
+                    ship(p, h, p, chip_half(p, h), p)
+    sources = (1, 2) if relayed else tuple(range(1, n_chip))
     half = gw_in.shape[1] // 2
     for copy in gw_feat:
         copy.wait()
@@ -267,20 +316,22 @@
     gw_full[mine] = total_half
     back = remote(gw_full.at[mine], gw_full.at[mine], e_send.at[1], e_recv.at[1], rows=mate)
     back.start()
-    for p in range(1, n_chip):
-        to_chip[p].wait_recv()
+    for p in sources:
+        for h in (0, 1):
+            landed(p, h, chip_half(p, h))
     for i in range(blocks):
         total = terms_ref[me_r * blocks + i].astype(F32) + mate_in[0, i].astype(F32)
-        for p in range(1, n_chip):
+        for p in sources:
             total = total + chip_in[p, i].astype(F32)
         gf_ref[:, i * edge:(i + 1) * edge] = total
     for p in order:
         to_mate[p].wait_send()
-        if p:
-            to_chip[p].wait_send()
+    for copy in sent:
+        copy.wait_send()
     back.wait_send()
     remote(gw_full.at[other], gw_full.at[other], e_send.at[1], e_recv.at[1], rows=mate).wait_recv()
-    gw_out[...] = gw_full[...]
+    gw_out[...] = gw_full[:, :gw_out.shape[1]]
+    gb_out[...] = gw_full[:, gw_out.shape[1]:]
 
 
 def on_device(node_feats, tile_vals, tile_cols, weight, bias_vec, grad_out):
@@ -320,7 +371,7 @@
             pltpu.VMEM(parts, BF16),
             pltpu.VMEM(parts, BF16),
             dma((blocks,)),
-        ] + [dma((n_chip,))] * 4 + [dma((n_feat,))] * 8 + [dma((n_feat, pairs))] * 2,
+        ] + [dma((n_chip, 2))] * 4 + [dma((n_feat,))] * 8 + [dma((n_feat, pairs))] * 2,
         compiler_params=pltpu.CompilerParams(
             collective_id=0, has_side_effects=True, vmem_limit_bytes=VMEM_BYTES),
         cost_estimate=pl.CostEstimate(flops=flops, bytes_accessed=tile_bytes, transcendentals=0),
@@ -349,17 +400,19 @@
         name="spread_terms",
     )(cols, bm.reshape(blocks, feat_loc, edge), tile_vals)
 
-    grad_feats, activated, gw = pl.pallas_call(
+    grad_feats, activated, gw, gb = pl.pallas_call(
         functools.partial(collect_kernel, n_rows, n_feat),
         out_shape=(
             jax.ShapeDtypeStruct((feat_loc, blocks * edge), F32),
             jax.ShapeDtypeStruct((feat_loc, blocks * edge), BF16),
-            jax.ShapeDtypeStruct((feat_loc, wide), F32),
+            jax.ShapeDtypeStruct((feat_loc, feat), F32),
+            jax.ShapeDtypeStruct((feat_loc, edge), F32),
         ),
         in_specs=[vmem] * 3,
-        out_specs=(vmem,) * 3,
+        out_specs=(vmem,) * 4,
         scratch_shapes=[pltpu.VMEM((n_chip, blocks, feat_loc, edge), BF16)] * 3
         + [
+            pltpu.VMEM((2, blocks // 2, feat_loc, edge), BF16),
             pltpu.VMEM(parts, BF16),
             pltpu.VMEM((n_feat, feat_loc, wide), F32),
             pltpu.VMEM((feat_loc, wide), F32),
@@ -367,13 +420,13 @@
             pltpu.VMEM((n_chip, feat_loc // 2, wide), F32),
             pltpu.VMEM((feat_loc, wide), F32),
         ]
-        + [dma((n_chip,))] * 6 + [dma((n_feat,))] * 4 + [dma((2,))] * 2,
+        + [dma((n_chip,))] * 2 + [dma((n_chip, 2))] * 2 + [dma((n_chip,))] * 2 + [dma((n_feat,))] * 4 + [dma((2,))] * 2,
         compiler_params=pltpu.CompilerParams(
             collective_id=1, has_side_effects=True, vmem_limit_bytes=VMEM_BYTES),
         cost_estimate=pl.CostEstimate(flops=1, bytes_accessed=tile_bytes // 4, transcendentals=0),
         name="collect_terms",
     )(terms, act, gw)
-    grad_weight, grad_bias = gw[:, :feat].T, jnp.sum(gw[:, feat:], axis=1)
+    grad_weight, grad_bias = gw.T, jnp.sum(gb, axis=1)
     return activated, grad_feats, grad_weight, grad_bias
 
 

time: 121 us -> 110 us (0.909)
  Pallas kernels: 112 us -> 100 us
    pallas_call x1, Pallas kernels: 62.4 us -> 56.1 us  [on_device(): pl.pallas_call(functools.partial(forward_kernel, n_rows, n_feat), out_sha...]
    pallas_call x1, Pallas kernels: 36.1 us -> 30.5 us  [on_device(): pl.pallas_call(functools.partial(collect_kernel, n_rows, n_feat), out_sha...]
    transpose x1 -> x0, local copies, waits for them, and re-layouts: 1.47 us -> none  [on_device(): grad_weight, grad_bias = (gw[:, :feat].T, jnp.sum(gw[:, feat:], axis=1))]
    unnamed x2 -> x3, local copies, waits for them, and re-layouts: 4.14 us -> 5.61 us
where the time goes in v3:
time: 110 us; the launch traced here: 109 us
  Pallas kernels  100 us (91%)
  local copies, waits for them, and re-layouts  6.95 us (6%)
  other arithmetic  1.38 us (1%)
    pallas_call x1, Pallas kernels, on_device(): pl.pallas_call(functools.partial(forward_kernel, n_rows, n_feat), out_sha...  56.1 us
    pallas_call x1, Pallas kernels, on_device(): pl.pallas_call(functools.partial(collect_kernel, n_rows, n_feat), out_sha...  30.5 us
    pallas_call x1, Pallas kernels, on_device(): pl.pallas_call(functools.partial(spread_kernel, blocks, slots, edge, grou...  13.5 us
    unnamed x3, local copies, waits for them, and re-layouts  5.61 us

profile of v3, /device:TPU:0, one launch (start us, length us, event | category | flops | bytes accessed | tf_op | source)
XLA Modules:
  0.0 109.1 jit_solution(13121618935629840918)
XLA Ops:
  0.6 1.3 %broadcast_in_dim.2.bias_ref = f32[64,128]{1,0:T(8,128)} broadcast(f32[64]{0:T(128)} %param.10), dimensions={0} | broadcast | bytes 33024 | tf_op jit(solution)/shard_map/broadcast_in_dim | solution.py:380
  2.0 56.1 %aggregate_and_mix.1 = (bf16[4,8,64,128]{3,2,1,0:T(8,128)(2,1)}, bf16[4,8,64,128]{3,2,1,0:T(8,128)(2,1)}, f32[4,64,384]{2,1,0:T(8,128)}) custom-call(s32[16,32]{1,0:T(8,128)} %bitcast.6, bf16[64,4096]{1,0:T(8,128)(2,1)} %x_ref.1, bf16[64,4096]{1,0:T(8,128)(2,1)} %gout_ref.1, bf16[64,256]{1,0:T(8,128)(2,1)} %bitcast.8, f32[64,128]{1,0:T(8,128)} %broadcast_in_dim.2.bias_ref, ...), custom_call_target="tpu_custom_call" | custom-call | flops 1073741824 | bytes 16777216 | tf_op jit(solution)/shard_map/aggregate_and_mix/pallas_call | solution.py:353
  58.0 13.5 %spread_terms.1.terms_ref = bf16[256,64,128]{2,1,0:T(8,128)(2,1)} custom-call(s32[16,32]{1,0:T(8,128)} %bitcast.7, bf16[32,64,128]{2,1,0:T(8,128)(2,1)} %bitcast.4, bf16[32,16,128,128]{3,2,1,0:T(8,128)(2,1)} %tiles_ref.1), custom_call_target="tpu_custom_call" | custom-call | flops 1073741824 | bytes 16777216 | tf_op jit(solution)/shard_map/spread_terms/pallas_call | solution.py:385
  71.6 30.5 %collect_terms.1 = (f32[64,4096]{1,0:T(8,128)}, bf16[64,4096]{1,0:T(8,128)(2,1)}, f32[64,256]{1,0:T(8,128)}, f32[64,128]{1,0:T(8,128)}) custom-call(bf16[256,64,128]{2,1,0:T(8,128)(2,1)} %spread_terms.1.terms_ref, bf16[4,8,64,128]{3,2,1,0:T(8,128)(2,1)} %get-tuple-element.12.act_ref, f32[4,64,384]{2,1,0:T(8,128)} %get-tuple-element.13.gw_ref), custom_call_target="tpu_custom_call" | custom-call | flops 1 | bytes 4194304 | tf_op jit(solution)/shard_map/collect_terms/pallas_call | solution.py:403
  102.1 1.4 %reduce_sum.9 = f32[64]{0:T(128)} reduce(f32[64,128]{1,0:T(8,128)} %get-tuple-element.17, f32[]{:T(128)} %constant.0.clone.1), dimensions={1}, to_apply=%region_0.0 | reduce | flops 8128 | bytes 33028 | tf_op jit(solution)/shard_map/reduce_sum | solution.py:429
  103.4 1.9 %copy.13 = bf16[64,4096]{1,0:T(8,128)(2,1)} copy(bf16[64,4096]{1,0:T(8,128)(2,1)} %get-tuple-element.22) | data formatting | bytes 1048576
  105.3 2.3 %copy.14 = f32[64,4096]{1,0:T(8,128)} copy(f32[64,4096]{1,0:T(8,128)} %get-tuple-element.23) | data formatting | bytes 2097152
  107.6 1.5 %copy.15 = f32[256,64]{0,1:T(8,128)} copy(f32[256,64]{0,1:T(8,128)} %bitcast.5) | data formatting | bytes 131072
